TPU v7x, 256 devices: a whole 4x4x8 slice. The times are simulated.
256 devices in a mesh: row: 16 (over y_hi, x, core), rep: 16 (over y_lo, z).
Axes of the slice: x: 4, y: 4 (y_hi: 2, y_lo: 2; y = y_hi * 2 + y_lo), z: 8, core: 2. Of those that a mesh axis runs over, the one named last changes fastest.
Arguments:
- features: bfloat16 [65536, 512], P(('row', 'rep')), may hold values from -6 to 6
- tiles: bfloat16 [512, 8, 128, 128], P(('row', 'rep')), may hold values from -0.1875 to 0.1875
- columns: int32 [512, 8], P(('row', 'rep')), may hold values from 0 to 511, as said below
- w_aggregate: bfloat16 [512, 512], replicated, may hold values from -0.25 to 0.25
- w_self: bfloat16 [512, 512], replicated, may hold values from -0.25 to 0.25
- w_middle: bfloat16 [512, 512], replicated, may hold values from -0.25 to 0.25
- w_output: bfloat16 [512, 512], replicated, may hold values from -0.25 to 0.25
- cotangent: bfloat16 [65536, 512], P(('row', 'rep')), may hold values from -6 to 6
Outputs:
- updated: bfloat16 [65536, 512], P(('row', 'rep'))
- grad_features: bfloat16 [65536, 512], P(('row', 'rep'))
- grad_output: float32 [512, 512], P('rep')
- grad_middle: float32 [512, 512], P('rep')
- grad_aggregate: float32 [512, 512], P('rep')
- grad_self: float32 [512, 512], P('rep')
Inputs may be any that keep to these rules, and one draw needn't show every extreme that they name: `columns`: row group g holds row blocks g * 32 to (g + 1) * 32 - 1, for g < 16. Every column block named by a row block of group g lies in group g - 1, g or g + 1, taken modulo 16; every row block names each of these three groups at least once. Column blocks may repeat within a row block.
All inputs are finite; a program needn't handle non-finite values.
Results may differ from a plain program's by a relative error of at most 0.015.
Values may be sent and summed in bfloat16 or wider, within the bound.
A program may use at most 192 MiB of HBM per device.

v0:
```python
import math
import jax
import jax.numpy as jnp
from jax import lax
from jax.sharding import PartitionSpec as P


def from_behind(value, axis, steps):
    count = lax.axis_size(axis)
    pairs = [(source, (source + steps) % count) for source in range(count)]
    return lax.ppermute(value, axis, pairs)


def silu_slope(value):
    sig = jax.nn.sigmoid(value)
    return sig * (1.0 + value * (1.0 - sig))


def times_transposed(left_operand, weight):
    return lax.dot_general(
        left_operand, weight, (((1,), (1,)), ((), ())), preferred_element_type=jnp.float32
    )


def local(features, tiles, columns, w_aggregate, w_self, w_middle, w_output, cotangent):
    blocks_dev, width_k, tile_size, _ = tiles.shape
    width = features.shape[1]
    groups = lax.axis_size("row")
    replicas = lax.axis_size("rep")
    panel_blocks = replicas * blocks_dev
    panel_rows = panel_blocks * tile_size
    group_id = lax.axis_index("row")
    slot_of = (columns // panel_blocks - group_id + 1) % groups
    window_index = slot_of * panel_blocks + columns % panel_blocks
    own_panel = lax.all_gather(features, "rep", axis=0, tiled=True)
    prior_panel = from_behind(own_panel, "row", 1)
    next_panel = from_behind(own_panel, "row", -1)
    window = jnp.concatenate([prior_panel, own_panel, next_panel], 0).reshape(
        3 * panel_blocks, tile_size, width
    )
    picked = window[window_index]
    summed = jnp.einsum("bkij,bkjf->bif", tiles, picked, preferred_element_type=jnp.float32)
    aggregate = summed.reshape(blocks_dev * tile_size, width).astype(jnp.bfloat16)
    pre_first = jnp.dot(aggregate, w_aggregate, preferred_element_type=jnp.float32) + jnp.dot(
        features, w_self, preferred_element_type=jnp.float32
    )
    first = jax.nn.silu(pre_first).astype(jnp.bfloat16)
    pre_second = jnp.dot(first, w_middle, preferred_element_type=jnp.float32)
    second = jax.nn.silu(pre_second).astype(jnp.bfloat16)
    updated = (
        features.astype(jnp.float32) + jnp.dot(second, w_output, preferred_element_type=jnp.float32)
    ).astype(jnp.bfloat16)
    delta_second = (times_transposed(cotangent, w_output) * silu_slope(pre_second)).astype(
        jnp.bfloat16
    )
    delta_first = (times_transposed(delta_second, w_middle) * silu_slope(pre_first)).astype(
        jnp.bfloat16
    )
    delta_aggregate = times_transposed(delta_first, w_aggregate).astype(jnp.bfloat16)
    delta_blocks = delta_aggregate.reshape(blocks_dev, tile_size, width)
    messages = jnp.einsum("bkji,bjf->bkif", tiles, delta_blocks, preferred_element_type=jnp.float32)
    spread = jnp.zeros((3 * panel_blocks, tile_size, width), jnp.float32)
    spread = spread.at[window_index.reshape(-1)].add(messages.reshape(-1, tile_size, width))
    spread = spread.reshape(3 * panel_rows, width)
    prior_part = spread[:panel_rows]
    own_part = spread[panel_rows : 2 * panel_rows]
    next_part = spread[2 * panel_rows :]
    from_next = from_behind(prior_part.astype(jnp.bfloat16), "row", -1).astype(prior_part.dtype)
    from_prior = from_behind(next_part.astype(jnp.bfloat16), "row", 1).astype(next_part.dtype)
    returned = lax.psum_scatter(
        (own_part + from_next + from_prior).astype(jnp.bfloat16),
        "rep",
        scatter_dimension=0,
        tiled=True,
    ).astype(jnp.float32)
    grad_features = (
        cotangent.astype(jnp.float32) + times_transposed(delta_first, w_self) + returned
    ).astype(jnp.bfloat16)
    total_nodes = features.shape[0] * groups * replicas
    scale = 1.0 / math.sqrt(total_nodes)
    local_output = jnp.dot(second.T, cotangent, preferred_element_type=jnp.float32)
    local_middle = jnp.dot(first.T, delta_second, preferred_element_type=jnp.float32)
    local_aggregate = jnp.dot(aggregate.T, delta_first, preferred_element_type=jnp.float32)
    local_self = jnp.dot(features.T, delta_first, preferred_element_type=jnp.float32)
    share_rows = width // replicas
    totals = lax.psum((local_output, local_middle, local_aggregate, local_self), ("row", "rep"))
    start_row = lax.axis_index("rep") * share_rows
    totals = tuple(
        (lax.dynamic_slice_in_dim(member, start_row, share_rows, 0) for member in totals)
    )
    return (
        updated,
        grad_features,
        totals[0] * scale,
        totals[1] * scale,
        totals[2] * scale,
        totals[3] * scale,
    )


def solution(mesh):
    placed = (
        P(("row", "rep"), None),
        P(("row", "rep"), None, None, None),
        P(("row", "rep"), None),
        P(),
        P(),
        P(),
        P(),
        P(("row", "rep"), None),
    )
    return jax.shard_map(
        local,
        mesh=mesh,
        in_specs=placed,
        out_specs=(
            P(("row", "rep"), None),
            P(("row", "rep"), None),
            P("rep", None),
            P("rep", None),
            P("rep", None),
            P("rep", None),
        ),
        check_vma=False,
    )
```

profile of v0, /device:TPU:4, one launch (start us, length us, event | category | flops | bytes accessed | tf_op | source)
XLA Modules:
  0.0 576.8 jit_solution(3026869364455568108)
XLA Ops:
  7.2 0.0 copy-start
  7.2 0.0 all-gather.2.cloned.1.call-start
  7.2 0.7 all-gather.2.cloned.1.call-update
  7.9 0.0 all-reduce.3.cloned.1.call-start
  8.0 81.7 %all-gather.2.cloned.1.call-done = bf16[4096,512]{1,0:T(8,128)(2,1)} async-done(((bf16[256,512]{1,0:T(8,128)(2,1)}), bf16[4096,512]{1,0:T(8,128)(2,1)}) %all-gather.2.cloned.1.call-update) | async-done | bytes 4194320 | tf_op jit(solution)/shard_map/all_gather | solution.py:35
  89.6 0.5 collective-permute-start
  90.1 0.7 compare_select_fusion
  90.8 0.1 reshape.66
  90.9 0.1 reshape.61
  91.0 45.0 %collective-permute-done.1 = bf16[4096,512]{1,0:T(8,128)(2,1)} collective-permute-done((bf16[4096,512]{1,0:T(8,128)(2,1)}, bf16[4096,512]{1,0:T(8,128)(2,1)}, u32[]{:S(2)}, u32[]{:S(2)}) %collective-permute-start.1) | collective-permute-done | bytes 4194336 | tf_op jit(solution)/shard_map/ppermute | solution.py:11
  136.0 1.9 collective-permute-done
  137.9 15.9 %pad_maximum_fusion = bf16[12288,512]{1,0:T(8,128)(2,1)} fusion(bf16[4096,512]{1,0:T(8,128)(2,1)} %collective-permute-done.1, bf16[4096,512]{1,0:T(8,128)(2,1)} %all-gather.2.cloned.1.call-done, bf16[4096,512]{1,0:T(8,128)(2,1)} %collective-permute-done), kind=kLoop, calls=%fused_computation.2 | loop fusion | flops 37748736 | bytes 25165824 | tf_op jit(solution)/shard_map/concatenate | solution.py:38
  153.8 5.3 gather_fusion
  159.1 0.0 copy-start.3
  159.2 0.0 copy-start.8
  159.2 0.4 fusion.2
  159.6 1.4 fusion.15
  161.0 0.3 convolution_add_fusion.2
  161.3 0.3 fusion.12
  161.7 0.4 fusion.4
  162.1 0.7 copy-done.10
  162.8 0.4 fusion.5
  163.2 0.3 convolution_convert_fusion
  163.5 2.7 fusion.16
  166.2 5.4 copy.15
  171.6 11.5 %broadcast_in_dim.8 = f32[96,128,512]{2,1,0:T(8,128)} broadcast(f32[]{:T(128)} %constant.62.clone.1), dimensions={} | broadcast | bytes 25165828 | tf_op jit(solution)/shard_map/broadcast_in_dim | solution.py:62
  183.1 9.6 %scatter_fusion = f32[96,128,512]{2,1,0:T(8,128)} fusion(f32[96,128,512]{2,1,0:T(8,128)} %broadcast_in_dim.8, s32[16]{0:T(128)S(1)} %fusion.9, f32[16,128,512]{2,1,0:T(8,128)} %copy.15), kind=kCustom, calls=%fused_computation.1 | custom fusion | flops 1048576 | bytes 12582976 | tf_op jit(solution)/shard_map/scatter-add | solution.py:63
  192.7 9.3 %convert.4 = bf16[96,128,512]{2,1,0:T(8,128)(2,1)S(1)} convert(f32[96,128,512]{2,1,0:T(8,128)} %scatter_fusion) | non-fusion elementwise | flops 6291456 | bytes 37748736 | tf_op jit(solution)/shard_map/convert.1
  202.0 3.5 fusion.14
  205.5 1.7 collective-permute-start.2
  207.3 1.3 fusion.17
  208.6 1.4 convolution_bitcast_fusion
  210.0 1.3 fusion.11
  211.3 1.4 fusion.10
  212.7 0.0 all-reduce.3.cloned.1.call-update
  212.7 0.0 reduce-scatter.2.cloned.1.call-start
  212.8 8.2 %slice.22 = f32[32,128,512]{2,1,0:T(8,128)} slice(f32[96,128,512]{2,1,0:T(8,128)} %scatter_fusion), slice={[32:64], [0:128], [0:512]} | slice | bytes 16777216 | tf_op jit(solution)/shard_map/slice | solution.py:66
  221.0 36.8 %collective-permute-done.3 = bf16[4096,512]{1,0:T(8,128)(2,1)} collective-permute-done((bf16[4096,512]{1,0:T(8,128)(2,1)}, bf16[4096,512]{1,0:T(8,128)(2,1)}, u32[]{:S(2)}, u32[]{:S(2)}) %collective-permute-start.3) | collective-permute-done | bytes 4194336 | tf_op jit(solution)/shard_map/ppermute | solution.py:11
  257.8 9.7 %fusion.1 = bf16[4096,512]{1,0:T(8,128)(2,1)} fusion(f32[32,128,512]{2,1,0:T(8,128)} %slice.22, bf16[4096,512]{1,0:T(8,128)(2,1)} %collective-permute-done.3, bf16[4096,512]{1,0:T(8,128)(2,1)} %collective-permute-done.2), kind=kLoop, calls=%fused_computation.5 | loop fusion | flops 10485760 | bytes 20971520 | tf_op jit(solution)/shard_map/convert_element_type | solution.py:71
  267.5 0.0 reduce-scatter.2.cloned.1.call-update
  267.5 1.0 copy-done.9
  268.5 1.0 fusion.3
  269.6 0.3 convolution_add_fusion
  269.9 216.6 %all-reduce.3.cloned.1.call-done = (f32[512,512]{1,0:T(8,128)}, f32[512,512]{1,0:T(8,128)}, f32[512,512]{1,0:T(8,128)}, f32[512,512]{1,0:T(8,128)}) async-done(((f32[512,512]{1,0:T(8,128)}, f32[512,512]{1,0:T(8,128)}, f32[512,512]{1,0:T(8,128)}, f32[512,512]{1,0:T(8,128)}), (f32[512,512]{1,0:T(8,128)}, f32[512,512]{1,0:T(8,128)}, f32[512,512]{1,0:T(8,128)}, ...) | async-done | bytes 4194320 | tf_op jit(solution)/shard_map/psum | solution.py:86
  486.5 1.5 dynamic-slice_multiply_fusion.2
  488.0 1.5 dynamic-slice_multiply_fusion
  489.6 79.0 %reduce-scatter.2.cloned.1.call-done = bf16[256,512]{1,0:T(8,128)(2,1)} async-done(((bf16[4096,512]{1,0:T(8,128)(2,1)}), bf16[256,512]{1,0:T(8,128)(2,1)}) %reduce-scatter.2.cloned.1.call-update) | async-done | bytes 262160 | tf_op jit(solution)/shard_map/reduce_scatter | solution.py:70
  568.6 1.7 add_convert_fusion
  (24 shorter events, 0.1 us)
Async XLA Ops:
  7.2 152.0 %copy-start = (bf16[2,8,128,128]{3,2,1,0:T(8,128)(2,1)S(1)}, bf16[2,8,128,128]{3,2,1,0:T(8,128)(2,1)}, u32[]{:S(2)}) copy-start(bf16[2,8,128,128]{3,2,1,0:T(8,128)(2,1)} %param.9) | copy-start | bytes 1572868
  7.2 82.4 %all-gather.2.cloned.1.call-start = ((), (), s32[]{:S(2)}) async-start(), calls=%async_computation.1 | async-start | bytes 4456448 | tf_op jit(solution)/shard_map/all_gather | solution.py:35
  7.9 478.6 %all-reduce.3.cloned.1.call-start = ((), (), s32[]{:S(2)}) async-start(), calls=%async_computation.3 | async-start | bytes 8388608 | tf_op jit(solution)/shard_map/psum | solution.py:86
  89.6 46.3 %collective-permute-start.1 = (bf16[4096,512]{1,0:T(8,128)(2,1)}, bf16[4096,512]{1,0:T(8,128)(2,1)}, u32[]{:S(2)}, u32[]{:S(2)}) collective-permute-start(bf16[4096,512]{1,0:T(8,128)(2,1)} %all-gather.2.cloned.1.call-done), channel_id=1, source_target_pairs={{0,240},{16,0},{32,16},{48,32},{64,48},{80,64},{96,80},{112,96},{1... | collective-permute-start | bytes 12582920 | tf_op jit(solution)/shard_map/ppermute | solution.py:11
  89.6 48.2 %collective-permute-start = (bf16[4096,512]{1,0:T(8,128)(2,1)}, bf16[4096,512]{1,0:T(8,128)(2,1)}, u32[]{:S(2)}, u32[]{:S(2)}) collective-permute-start(bf16[4096,512]{1,0:T(8,128)(2,1)} %all-gather.2.cloned.1.call-done), channel_id=1, source_target_pairs={{0,16},{16,32},{32,48},{48,64},{64,80},{80,96},{96,112},{112,128},... | collective-permute-start | bytes 12582920 | tf_op jit(solution)/shard_map/ppermute | solution.py:11
  153.8 7.2 %copy-start.2 = (bf16[256,512]{1,0:T(8,128)(2,1)S(1)}, bf16[256,512]{1,0:T(8,128)(2,1)}, u32[]{:S(2)}) copy-start(bf16[256,512]{1,0:T(8,128)(2,1)} %param.8) | copy-start | bytes 786436
  159.1 1.9 copy-start.3
  159.1 2.2 copy-start.7
  159.1 2.5 copy-start.6
  159.2 2.5 copy-start.8
  161.7 1.5 copy-start.5
  162.1 0.7 copy-start.10
  202.0 8.0 %copy-start.11 = (bf16[256,512]{1,0:T(8,128)(2,1)S(1)}, bf16[256,512]{1,0:T(8,128)(2,1)}, u32[]{:S(2)}) copy-start(bf16[256,512]{1,0:T(8,128)(2,1)} %copy-done.10) | copy-start | bytes 786436
  205.5 52.3 %collective-permute-start.3 = (bf16[4096,512]{1,0:T(8,128)(2,1)}, bf16[4096,512]{1,0:T(8,128)(2,1)}, u32[]{:S(2)}, u32[]{:S(2)}) collective-permute-start(bf16[4096,512]{1,0:T(8,128)(2,1)} %bitcast.13), channel_id=1, source_target_pairs={{0,16},{16,32},{32,48},{48,64},{64,80},{80,96},{96,112},{112,128},... | collective-permute-start | bytes 12582920 | tf_op jit(solution)/shard_map/ppermute | solution.py:11
  205.5 52.3 %collective-permute-start.2 = (bf16[4096,512]{1,0:T(8,128)(2,1)}, bf16[4096,512]{1,0:T(8,128)(2,1)}, u32[]{:S(2)}, u32[]{:S(2)}) collective-permute-start(bf16[4096,512]{1,0:T(8,128)(2,1)} %bitcast.12), channel_id=1, source_target_pairs={{0,240},{16,0},{32,16},{48,32},{64,48},{80,64},{96,80},{112,96},{1... | collective-permute-start | bytes 12582920 | tf_op jit(solution)/shard_map/ppermute | solution.py:11
  212.7 355.9 %reduce-scatter.2.cloned.1.call-start = ((), (), s32[]{:S(2)}) async-start(), calls=%async_computation.2 | async-start | bytes 4456448 | tf_op jit(solution)/shard_map/reduce_scatter | solution.py:70
  267.5 1.0 copy-start.9
  267.5 2.1 copy-start.4
  267.5 302.8 %copy-start.1 = (bf16[2,8,128,128]{3,2,1,0:T(8,128)(2,1)S(1)}, bf16[2,8,128,128]{3,2,1,0:T(8,128)(2,1)}, u32[]{:S(2)}) copy-start(bf16[2,8,128,128]{3,2,1,0:T(8,128)(2,1)} %param.9) | copy-start | bytes 1572868
Sparse Core Ops, SparseCore 0:
  9.8 79.7 all-gather.1
  212.8 273.6 all-reduce.2
  489.2 79.3 reduce-scatter.1
where the time goes:
time: 577 us
  waiting for transfers between devices  462 us (80%)
  other arithmetic  50 us (9%)
  local copies, waits for them, and re-layouts  35.9 us (6%)
  between operations  14 us (2%)
  matrix products  13 us (2%)
    psum x1, waiting for transfers between devices, local(): lax.psum((local_output, local_middle, local_aggregate, local_self), ('row...  217 us
    ppermute x4, waiting for transfers between devices, from_behind(): return lax.ppermute(value, axis, pairs)  83.7 us
    all_gather x1, waiting for transfers between devices, local(): own_panel = lax.all_gather(features, 'rep', axis=0, tiled=True)  81.7 us
    reduce_scatter x1, waiting for transfers between devices, local(): lax.psum_scatter((own_part + from_next + from_prior).astype(jnp.bfloat16)...  79 us
    concatenate x1, other arithmetic, local(): jnp.concatenate([prior_panel, own_panel, next_panel], 0)  15.9 us
  transfers between devices with their start and end apart: 7, of which 6 were waited for; matrix products, arithmetic and copies ran while one was open for 5% of the time, Pallas kernels for 0%

commit v1 on v0

--- a/solution.py
+++ b/solution.py
@@ -83,7 +83,9 @@
     local_aggregate = jnp.dot(aggregate.T, delta_first, preferred_element_type=jnp.float32)
     local_self = jnp.dot(features.T, delta_first, preferred_element_type=jnp.float32)
     share_rows = width // replicas
-    totals = lax.psum((local_output, local_middle, local_aggregate, local_self), ("row", "rep"))
+    totals = lax.psum(
+        lax.psum((local_output, local_middle, local_aggregate, local_self), "row"), "rep"
+    )
     start_row = lax.axis_index("rep") * share_rows
     totals = tuple(
         (lax.dynamic_slice_in_dim(member, start_row, share_rows, 0) for member in totals)

time: 577 us -> 577 us (level)
    psum x1 -> x2, waiting for transfers between devices: 217 us -> 255 us  [the longest x1 144 us: local(): lax.psum(lax.psum((local_output, local_middle, local_aggregate, local_sel...]
    ppermute x4, waiting for transfers between devices: 83.7 us -> 46.9 us  [from_behind(): return lax.ppermute(value, axis, pairs)]
  transfers between devices with their start and end apart: 7 -> 8, of which waited for: 6 -> 6; matrix products, arithmetic and copies ran while one was open for 5% -> 11% of each run, Pallas kernels for 0% -> 0%
where the time goes in v1:
time: 577 us; the launch traced here: 576 us
  waiting for transfers between devices  461 us (80%)
  other arithmetic  50 us (9%)
  local copies, waits for them, and re-layouts  35.6 us (6%)
  between operations  13.9 us (2%)
  matrix products  13 us (2%)
    psum x1, waiting for transfers between devices, local(): lax.psum(lax.psum((local_output, local_middle, local_aggregate, local_sel...  144 us
    psum x1, waiting for transfers between devices, local(): lax.psum((local_output, local_middle, local_aggregate, local_self), 'row')  111 us
    all_gather x1, waiting for transfers between devices, local(): own_panel = lax.all_gather(features, 'rep', axis=0, tiled=True)  81.7 us
    reduce_scatter x1, waiting for transfers between devices, local(): lax.psum_scatter((own_part + from_next + from_prior).astype(jnp.bfloat16)...  77.2 us
    ppermute x4, waiting for transfers between devices, from_behind(): return lax.ppermute(value, axis, pairs)  46.9 us
    concatenate x1, other arithmetic, local(): jnp.concatenate([prior_panel, own_panel, next_panel], 0)  15.9 us
    broadcast_in_dim x1, local copies, waits for them, and re-layouts, local(): spread = jnp.zeros((3 * panel_blocks, tile_size, width), jnp.float32)  11.9 us
  transfers between devices with their start and end apart: 8, of which 6 were waited for; matrix products, arithmetic and copies ran while one was open for 11% of the time, Pallas kernels for 0%

profile of v1, /device:TPU:4, one launch (start us, length us, event | category | flops | bytes accessed | tf_op | source)
XLA Modules:
  0.0 576.2 jit_solution(3201261502232360988)
XLA Ops:
  7.2 0.0 copy-start
  7.2 0.0 all-gather.2.cloned.1.call-start
  7.2 0.7 all-gather.2.cloned.1.call-update
  7.9 0.0 all-reduce.7.cloned.1.call-start
  8.0 81.7 %all-gather.2.cloned.1.call-done = bf16[4096,512]{1,0:T(8,128)(2,1)} async-done(((bf16[256,512]{1,0:T(8,128)(2,1)}), bf16[4096,512]{1,0:T(8,128)(2,1)}) %all-gather.2.cloned.1.call-update) | async-done | bytes 4194320 | tf_op jit(solution)/shard_map/all_gather | solution.py:35
  89.6 0.5 collective-permute-start
  90.1 0.7 compare_select_fusion
  90.8 0.1 reshape.66
  90.9 45.0 %collective-permute-done.1 = bf16[4096,512]{1,0:T(8,128)(2,1)} collective-permute-done((bf16[4096,512]{1,0:T(8,128)(2,1)}, bf16[4096,512]{1,0:T(8,128)(2,1)}, u32[]{:S(2)}, u32[]{:S(2)}) %collective-permute-start.1) | collective-permute-done | bytes 4194336 | tf_op jit(solution)/shard_map/ppermute | solution.py:11
  136.0 1.9 collective-permute-done
  137.9 15.9 %pad_maximum_fusion = bf16[12288,512]{1,0:T(8,128)(2,1)} fusion(bf16[4096,512]{1,0:T(8,128)(2,1)} %collective-permute-done.1, bf16[4096,512]{1,0:T(8,128)(2,1)} %all-gather.2.cloned.1.call-done, bf16[4096,512]{1,0:T(8,128)(2,1)} %collective-permute-done), kind=kLoop, calls=%fused_computation.2 | loop fusion | flops 37748736 | bytes 25165824 | tf_op jit(solution)/shard_map/concatenate | solution.py:38
  153.8 5.3 gather_fusion
  159.1 0.0 copy-start.7
  159.2 0.4 fusion.2
  159.6 1.3 fusion.15
  161.0 0.3 convolution_add_fusion.2
  161.3 0.3 fusion.12
  161.7 0.4 fusion.4
  162.1 0.4 fusion.5
  162.4 1.3 fusion.11
  163.8 1.4 fusion.10
  165.2 1.3 fusion.17
  166.5 1.3 convolution_bitcast_fusion
  167.8 0.0 all-reduce.7.cloned.1.call-update
  167.9 0.0 all-reduce.5.cloned.1.call-start
  167.9 0.1 reshape.61
  168.0 0.3 convolution_convert_fusion
  168.3 2.7 fusion.16
  171.0 5.4 copy.15
  176.4 11.9 %broadcast_in_dim.8 = f32[96,128,512]{2,1,0:T(8,128)} broadcast(f32[]{:T(128)} %constant.62.clone.1), dimensions={} | broadcast | bytes 25165828 | tf_op jit(solution)/shard_map/broadcast_in_dim | solution.py:62
  188.2 9.7 %scatter_fusion = f32[96,128,512]{2,1,0:T(8,128)} fusion(f32[96,128,512]{2,1,0:T(8,128)} %broadcast_in_dim.8, s32[16]{0:T(128)S(1)} %fusion.9, f32[16,128,512]{2,1,0:T(8,128)} %copy.15), kind=kCustom, calls=%fused_computation.1 | custom fusion | flops 1048576 | bytes 12582976 | tf_op jit(solution)/shard_map/scatter-add | solution.py:63
  197.9 9.3 %convert.4 = bf16[96,128,512]{2,1,0:T(8,128)(2,1)S(1)} convert(f32[96,128,512]{2,1,0:T(8,128)} %scatter_fusion) | non-fusion elementwise | flops 6291456 | bytes 37748736 | tf_op jit(solution)/shard_map/convert.1
  207.3 3.6 fusion.14
  210.9 1.7 collective-permute-start.2
  212.6 110.6 %all-reduce.7.cloned.1.call-done = (f32[512,512]{1,0:T(8,128)}, f32[512,512]{1,0:T(8,128)}, f32[512,512]{1,0:T(8,128)}, f32[512,512]{1,0:T(8,128)}) async-done(((f32[512,512]{1,0:T(8,128)}, f32[512,512]{1,0:T(8,128)}, f32[512,512]{1,0:T(8,128)}, f32[512,512]{1,0:T(8,128)}), (f32[512,512]{1,0:T(8,128)}, f32[512,512]{1,0:T(8,128)}, f32[512,512]{1,0:T(8,128)}, ...) | async-done | bytes 4194320 | tf_op jit(solution)/shard_map/psum | solution.py:87
  323.2 0.0 all-reduce.5.cloned.1.call-update
  323.2 0.0 reduce-scatter.2.cloned.1.call-start
  323.3 8.2 %slice.22 = f32[32,128,512]{2,1,0:T(8,128)} slice(f32[96,128,512]{2,1,0:T(8,128)} %scatter_fusion), slice={[32:64], [0:128], [0:512]} | slice | bytes 16777216 | tf_op jit(solution)/shard_map/slice | solution.py:66
  331.5 9.5 %fusion.1 = bf16[4096,512]{1,0:T(8,128)(2,1)} fusion(f32[32,128,512]{2,1,0:T(8,128)} %slice.22, bf16[4096,512]{1,0:T(8,128)(2,1)} %collective-permute-done.3, bf16[4096,512]{1,0:T(8,128)(2,1)} %collective-permute-done.2), kind=kLoop, calls=%fused_computation.5 | loop fusion | flops 10485760 | bytes 20971520 | tf_op jit(solution)/shard_map/convert_element_type | solution.py:71
  341.0 0.0 reduce-scatter.2.cloned.1.call-update
  341.1 1.0 copy-done.9
  342.1 1.0 fusion.3
  343.1 0.3 convolution_add_fusion
  343.5 144.3 %all-reduce.5.cloned.1.call-done = (f32[512,512]{1,0:T(8,128)}, f32[512,512]{1,0:T(8,128)}, f32[512,512]{1,0:T(8,128)}, f32[512,512]{1,0:T(8,128)}) async-done(((f32[512,512]{1,0:T(8,128)}, f32[512,512]{1,0:T(8,128)}, f32[512,512]{1,0:T(8,128)}, f32[512,512]{1,0:T(8,128)}), (f32[512,512]{1,0:T(8,128)}, f32[512,512]{1,0:T(8,128)}, f32[512,512]{1,0:T(8,128)}, ...) | async-done | bytes 4194320 | tf_op jit(solution)/shard_map/psum | solution.py:86
  487.7 1.5 dynamic-slice_multiply_fusion.2
  489.3 1.5 dynamic-slice_multiply_fusion
  490.8 77.2 %reduce-scatter.2.cloned.1.call-done = bf16[256,512]{1,0:T(8,128)(2,1)} async-done(((bf16[4096,512]{1,0:T(8,128)(2,1)}), bf16[256,512]{1,0:T(8,128)(2,1)}) %reduce-scatter.2.cloned.1.call-update) | async-done | bytes 262160 | tf_op jit(solution)/shard_map/reduce_scatter | solution.py:70
  568.0 1.7 add_convert_fusion
  (23 shorter events, 0.1 us)
Async XLA Ops:
  7.2 152.0 %copy-start = (bf16[2,8,128,128]{3,2,1,0:T(8,128)(2,1)S(1)}, bf16[2,8,128,128]{3,2,1,0:T(8,128)(2,1)}, u32[]{:S(2)}) copy-start(bf16[2,8,128,128]{3,2,1,0:T(8,128)(2,1)} %param.9) | copy-start | bytes 1572868
  7.2 82.4 %all-gather.2.cloned.1.call-start = ((), (), s32[]{:S(2)}) async-start(), calls=%async_computation.1 | async-start | bytes 4456448 | tf_op jit(solution)/shard_map/all_gather | solution.py:35
  7.9 315.3 %all-reduce.7.cloned.1.call-start = ((), (), s32[]{:S(2)}) async-start(), calls=%async_computation.4 | async-start | bytes 8388608 | tf_op jit(solution)/shard_map/psum | solution.py:87
  89.6 46.3 %collective-permute-start.1 = (bf16[4096,512]{1,0:T(8,128)(2,1)}, bf16[4096,512]{1,0:T(8,128)(2,1)}, u32[]{:S(2)}, u32[]{:S(2)}) collective-permute-start(bf16[4096,512]{1,0:T(8,128)(2,1)} %all-gather.2.cloned.1.call-done), channel_id=1, source_target_pairs={{0,240},{16,0},{32,16},{48,32},{64,48},{80,64},{96,80},{112,96},{1... | collective-permute-start | bytes 12582920 | tf_op jit(solution)/shard_map/ppermute | solution.py:11
  89.6 48.2 %collective-permute-start = (bf16[4096,512]{1,0:T(8,128)(2,1)}, bf16[4096,512]{1,0:T(8,128)(2,1)}, u32[]{:S(2)}, u32[]{:S(2)}) collective-permute-start(bf16[4096,512]{1,0:T(8,128)(2,1)} %all-gather.2.cloned.1.call-done), channel_id=1, source_target_pairs={{0,16},{16,32},{32,48},{48,64},{64,80},{80,96},{96,112},{112,128},... | collective-permute-start | bytes 12582920 | tf_op jit(solution)/shard_map/ppermute | solution.py:11
  153.8 7.2 %copy-start.2 = (bf16[256,512]{1,0:T(8,128)(2,1)S(1)}, bf16[256,512]{1,0:T(8,128)(2,1)}, u32[]{:S(2)}) copy-start(bf16[256,512]{1,0:T(8,128)(2,1)} %param.8) | copy-start | bytes 786436
  153.8 7.2 %copy-start.3 = (bf16[512,512]{1,0:T(8,128)(2,1)S(1)}, bf16[512,512]{1,0:T(8,128)(2,1)}, u32[]{:S(2)}) copy-start(bf16[512,512]{1,0:T(8,128)(2,1)} %param.12) | copy-start | bytes 1572868
  159.1 2.2 copy-start.7
  159.2 2.5 copy-start.5
  159.2 2.5 copy-start.8
  165.2 2.8 copy-start.4
  167.9 319.9 %all-reduce.5.cloned.1.call-start = ((), (), s32[]{:S(2)}) async-start(), calls=%async_computation.3 | async-start | bytes 8388608 | tf_op jit(solution)/shard_map/psum | solution.py:86
  210.8 120.6 %collective-permute-start.3 = (bf16[4096,512]{1,0:T(8,128)(2,1)}, bf16[4096,512]{1,0:T(8,128)(2,1)}, u32[]{:S(2)}, u32[]{:S(2)}) collective-permute-start(bf16[4096,512]{1,0:T(8,128)(2,1)} %bitcast.13), channel_id=1, source_target_pairs={{0,16},{16,32},{32,48},{48,64},{64,80},{80,96},{96,112},{112,128},... | collective-permute-start | bytes 12582920 | tf_op jit(solution)/shard_map/ppermute | solution.py:11
  210.9 120.6 %collective-permute-start.2 = (bf16[4096,512]{1,0:T(8,128)(2,1)}, bf16[4096,512]{1,0:T(8,128)(2,1)}, u32[]{:S(2)}, u32[]{:S(2)}) collective-permute-start(bf16[4096,512]{1,0:T(8,128)(2,1)} %bitcast.12), channel_id=1, source_target_pairs={{0,240},{16,0},{32,16},{48,32},{64,48},{80,64},{96,80},{112,96},{1... | collective-permute-start | bytes 12582920 | tf_op jit(solution)/shard_map/ppermute | solution.py:11
  323.2 244.7 %reduce-scatter.2.cloned.1.call-start = ((), (), s32[]{:S(2)}) async-start(), calls=%async_computation.2 | async-start | bytes 4456448 | tf_op jit(solution)/shard_map/reduce_scatter | solution.py:70
  341.0 1.0 copy-start.9
  341.0 2.1 copy-start.6
  341.1 228.6 %copy-start.1 = (bf16[2,8,128,128]{3,2,1,0:T(8,128)(2,1)S(1)}, bf16[2,8,128,128]{3,2,1,0:T(8,128)(2,1)}, u32[]{:S(2)}) copy-start(bf16[2,8,128,128]{3,2,1,0:T(8,128)(2,1)} %param.9) | copy-start | bytes 1572868
Sparse Core Ops, SparseCore 0:
  9.8 79.7 all-gather.1
  168.0 155.1 all-reduce.6
  326.1 161.5 all-reduce.4
  490.1 77.7 reduce-scatter.1
